TPU v7x, 256 devices: a whole 4x4x8 slice. The times are simulated.
256 devices in a mesh: seg: 64 (over y, x, z_lo), chan: 4 (over z_hi, core).
Axes of the slice: x: 4, y: 4, z: 8 (z_hi: 2, z_lo: 4; z = z_hi * 4 + z_lo), core: 2. Of those that a mesh axis runs over, the one named last changes fastest.
Arguments:
- raw: bfloat16 [5120, 262144], P('chan', 'seg'), may hold values from -6 to 6
- fir_taps: bfloat16 [256], replicated, may hold values from -0.375 to 0.375
- band_lo: int32 [1], replicated, may hold values from 4 to 16
- source_chan: int32 [256], replicated, may hold values from 0 to 5119
- dead_chan: int32 [64], replicated, may hold values from 0 to 5119
Outputs:
- stacked: bfloat16 [192, 2, 256, 5120], P('seg', None, None, 'chan')
All inputs are finite; a program needn't handle non-finite values.
Results may differ from a plain program's by a relative error of at most 0.0086.
Values may be sent and summed in bfloat16 or wider, within the bound.
A program may use at most 128 MiB of HBM per device.

v0:
```python
import math

import jax
import jax.numpy as jnp
from jax import lax
from jax.sharding import PartitionSpec as P

NFFT = 1024
DEC = 4
TAPS = 256
BIN_DEV = 3


def shifted(block, axis, distance):
    devices = range(lax.axis_size(axis))
    route = [(i - distance, i) for i in devices if i - distance in devices]
    return lax.ppermute(block, axis, route)


def filter_matrix(fir_taps, decim, taps):
    block_rows = 128 + taps // decim
    length = block_rows + 128
    padded = jnp.pad(fir_taps, (decim * (block_rows - 1), decim * length + decim))
    phases = []
    for phase_no in range(decim):
        begin = decim - 1 + taps - phase_no
        diagonal = padded[begin : begin + decim * length : decim]
        rolled = jnp.roll(diagonal, -(block_rows - 1))
        tiled = jnp.tile(rolled, block_rows)[: block_rows * (length - 1)]
        phases.append(tiled.reshape(block_rows, length - 1)[:, :128])
    return jnp.stack(phases, axis=1).reshape(decim * block_rows, 128)


def dft_table(band_lo, nbins, nfft):
    freq = band_lo[0] + lax.broadcasted_iota(jnp.int32, (nbins, nfft), 0)
    moment = lax.broadcasted_iota(jnp.int32, (nbins, nfft), 1)
    phase = (freq * moment % nfft).astype(jnp.float32) * (2.0 * math.pi / nfft)
    return jnp.concatenate([jnp.cos(phase), -jnp.sin(phase)], axis=0).astype(jnp.bfloat16)


def whiten(spec, alive, nbins):
    real = spec[:nbins]
    imag = spec[nbins:]
    power = real * real + imag * imag
    level = jnp.mean(power, axis=0, keepdims=True)
    factor = alive / jnp.sqrt(power + 0.1 * level + 1e-06)
    return jnp.stack([real * factor, imag * factor]).astype(jnp.bfloat16)


def correlate(block, sources, factor):
    left = jnp.concatenate([sources[:, 0], sources[:, 1]], axis=0)
    right_real = jnp.concatenate([block[:, 0], block[:, 1]], axis=0)
    right_imag = jnp.concatenate([block[:, 1], -block[:, 0]], axis=0)
    real = jnp.einsum("sbv,sbc->bvc", left, right_real, preferred_element_type=jnp.float32)
    imag = jnp.einsum("sbv,sbc->bvc", left, right_imag, preferred_element_type=jnp.float32)
    return (jnp.stack([real, imag], axis=1) * factor).astype(jnp.bfloat16)


def per_device(raw, fir_taps, band_lo, source_chan, dead_chan):
    chan_dev = raw.shape[0]
    samples = raw.shape[1]
    nbins = BIN_DEV * lax.axis_size("seg")
    factor = 1.0 / math.sqrt(lax.axis_size("seg"))
    tail = raw[:, samples - TAPS :]
    prior = shifted(tail, "seg", 1)
    extended = jnp.concatenate([prior, raw], axis=1)
    hmat = filter_matrix(fir_taps, DEC, TAPS)
    span = hmat.shape[0]
    stride = DEC * 128
    windows = jnp.stack(
        [extended[:, b * stride : b * stride + span] for b in range(NFFT // 128)], axis=1
    )
    trace = jnp.einsum("cbi,ij->cbj", windows, hmat, preferred_element_type=jnp.float32)
    trace = trace.reshape(chan_dev, NFFT).astype(jnp.bfloat16)
    table = dft_table(band_lo, nbins, NFFT)
    spec = jnp.einsum("kn,cn->kc", table, trace, preferred_element_type=jnp.float32)
    first = lax.axis_index("chan") * chan_dev
    global_chan = first + lax.broadcasted_iota(jnp.int32, (1, chan_dev), 1)
    alive = 1.0 - jnp.any(dead_chan[:, None] == global_chan, axis=0, keepdims=True).astype(
        jnp.float32
    )
    white = whiten(spec, alive, nbins)
    picker = (global_chan[0][:, None] == source_chan[None, :]).astype(jnp.bfloat16)
    picked = jnp.einsum("knc,cv->knv", white, picker, preferred_element_type=jnp.float32)
    summed = lax.psum(picked[None].astype(jnp.bfloat16), "chan")
    sources = lax.all_to_all(summed, "seg", split_axis=2, concat_axis=0, tiled=True)
    return correlate(
        lax.all_to_all(white[None], "seg", split_axis=2, concat_axis=0, tiled=True), sources, factor
    )


def solution(mesh):
    return jax.shard_map(
        per_device,
        mesh=mesh,
        in_specs=(P("chan", "seg"), P(), P(), P(), P()),
        out_specs=P("seg", None, None, "chan"),
        check_vma=False,
    )
```

profile of v0, /device:TPU:1, one launch (start us, length us, event | category | flops | bytes accessed | tf_op | source)
XLA Modules:
  0.0 173.4 jit_solution(11015482070662752424)
XLA Ops:
  6.5 1.1 slice.109
  7.7 4.4 %collective-permute-start = (bf16[1280,256]{1,0:T(8,128)(2,1)S(1)}, bf16[1280,256]{1,0:T(8,128)(2,1)S(1)}, u32[]{:S(2)}, u32[]{:S(2)}) collective-permute-start(bf16[1280,256]{1,0:T(8,128)(2,1)S(1)} %slice.109), channel_id=1, source_target_pairs={{0,4},{4,8},{8,12},{12,16},{16,20},{20,24},{24,28},{28,32},{32,36}... | collective-permute-start | bytes 1966088 | tf_op jit(solution)/shard_map/ppermute | solution.py:17
  12.1 0.7 pad.4
  12.8 0.2 slice.133
  13.1 0.2 slice.128
  13.4 0.2 slice.123
  13.8 0.2 slice.118
  14.2 0.2 tile.43
  14.4 0.4 reshape.79
  14.8 0.2 tile.41
  15.1 0.4 reshape.78
  15.4 0.1 pad_maximum_fusion.7
  15.5 0.2 tile.19
  15.7 0.4 reshape.77
  16.2 0.2 tile.17
  16.4 0.4 reshape.76
  16.9 0.2 copy.23
  17.7 0.1 compare_reduce_fusion
  17.9 4.3 %cosine_convert_fusion = (bf16[192,1024]{1,0:T(8,128)(2,1)S(1)}, bf16[192,1024]{1,0:T(8,128)(2,1)}) fusion(s32[192]{0:T(256)S(1)} %iota_add_fusion.1), kind=kLoop, calls=%fused_computation.46 | loop fusion | flops 3342336 | bytes 787200 | tf_op jit(solution)/shard_map/convert.8
  22.2 3.3 %collective-permute-done = bf16[1280,256]{1,0:T(8,128)(2,1)S(1)} collective-permute-done((bf16[1280,256]{1,0:T(8,128)(2,1)S(1)}, bf16[1280,256]{1,0:T(8,128)(2,1)S(1)}, u32[]{:S(2)}, u32[]{:S(2)}) %collective-permute-start) | collective-permute-done | bytes 655392 | tf_op jit(solution)/shard_map/ppermute | solution.py:17
  25.4 1.4 fusion.2
  26.9 0.2 bitcast_dynamic-update-slice_fusion.6
  27.1 0.2 bitcast_dynamic-update-slice_fusion.5
  27.3 0.2 bitcast_dynamic-update-slice_fusion.4
  27.6 0.2 bitcast_dynamic-update-slice_fusion.3
  27.8 0.2 bitcast_dynamic-update-slice_fusion.2
  28.0 0.2 bitcast_dynamic-update-slice_fusion.1
  28.2 0.2 bitcast_dynamic-update-slice_fusion
  28.4 5.5 %copy-done.1 = bf16[1280,8,768]{2,0,1:T(8,128)(2,1)} copy-done((bf16[1280,8,768]{2,0,1:T(8,128)(2,1)}, bf16[1280,8,768]{2,0,1:T(8,128)(2,1)S(1)}, u32[]{:S(2)}) %copy-start.1) | copy-done | bytes 15728664
  33.9 10.7 %convolution_convert_fusion = bf16[1280,8,128]{0,2,1:T(8,128)(2,1)S(1)} fusion(bf16[1280,8,768]{2,0,1:T(8,128)(2,1)} %copy-done.1, bf16[768,128,1]{1,0,2:T(8,128)(2,1)S(1)} %bitcast.85), kind=kOutput, calls=%fused_computation.2 | convolution fusion | flops 2014576640 | bytes 18546688 | tf_op jit(solution)/shard_map/cbi,ij->cbj/dot_general | solution.py:73
  44.6 2.2 %fusion.24 = f32[384,1280]{1,0:T(8,128)S(1)} fusion(bf16[1280,1024]{0,1:T(8,128)(2,1)S(1)} %bitcast.79, bf16[192,1024]{1,0:T(8,128)(2,1)} %get-tuple-element.12, bf16[192,1024]{1,0:T(8,128)(2,1)S(1)} %get-tuple-element.11), kind=kOutput, calls=%fused_computation.41 | convolution fusion | flops 1008205824 | bytes 5373952 | tf_op jit(solution)/shard_map/kn,cn->kc/dot_general | solution.py:76
  46.8 0.1 fusion.38
  47.0 0.3 multiply_convert_fusion.1
  47.3 1.2 fusion.9
  48.6 61.0 %all-reduce.3.cloned.1.call-done = bf16[1,2,192,256]{3,2,1,0:T(8,128)(2,1)} async-done(((bf16[1,2,192,256]{3,2,1,0:T(8,128)(2,1)}), bf16[1,2,192,256]{3,2,1,0:T(8,128)(2,1)}) %all-reduce.3.cloned.1.call-update) | async-done | bytes 196624 | tf_op jit(solution)/shard_map/psum | solution.py:85
  109.6 1.8 %copy.25 = bf16[1,2,192,256]{3,1,0,2:T(2,128)(2,1)} copy(bf16[1,2,192,256]{3,2,1,0:T(8,128)(2,1)} %all-reduce.3.cloned.1.call-done) | data formatting | bytes 393216 | tf_op jit(solution)/shard_map/psum | solution.py:85
  111.4 7.7 %all-to-all-start = ((bf16[1,2,192,256]{3,1,0,2:T(2,128)(2,1)}), bf16[1,2,192,256]{3,1,0,2:T(2,128)(2,1)S(1)}, u32[]{:S(2)}, u32[]{:S(2)}) async-start(bf16[1,2,192,256]{3,1,0,2:T(2,128)(2,1)} %copy.25), calls=%async_computation | async-start | bytes 393216 | tf_op jit(solution)/shard_map/all_to_all | solution.py:86
  119.1 0.1 pad_maximum_fusion.1
  119.2 2.0 %copy.27 = bf16[1,2,192,1280]{3,1,0,2:T(2,128)(2,1)} copy(bf16[1,2,192,1280]{3,2,1,0:T(8,128)(2,1)S(1)} %pad_maximum_fusion.1) | data formatting | bytes 1966080 | tf_op jit(solution)/shard_map/stack | solution.py:47
  121.2 8.2 %all-to-all-done = bf16[1,2,192,256]{3,1,0,2:T(2,128)(2,1)S(1)} async-done(((bf16[1,2,192,256]{3,1,0,2:T(2,128)(2,1)}), bf16[1,2,192,256]{3,1,0,2:T(2,128)(2,1)S(1)}, u32[]{:S(2)}, u32[]{:S(2)}) %all-to-all-start) | async-done | bytes 196640 | tf_op jit(solution)/shard_map/all_to_all | solution.py:86
  129.4 5.6 %all-to-all-start.1 = ((bf16[1,2,192,1280]{3,1,0,2:T(2,128)(2,1)}), bf16[1,2,192,1280]{3,1,0,2:T(2,128)(2,1)S(1)}, u32[]{:S(2)}, u32[]{:S(2)}) async-start(bf16[1,2,192,1280]{3,1,0,2:T(2,128)(2,1)} %copy.27), calls=%async_computation.1 | async-start | bytes 1966080 | tf_op jit(solution)/shard_map/all_to_all | solution.py:88
  135.0 0.3 copy.26
  135.3 26.7 %all-to-all-done.1 = bf16[1,2,192,1280]{3,1,0,2:T(2,128)(2,1)S(1)} async-done(((bf16[1,2,192,1280]{3,1,0,2:T(2,128)(2,1)}), bf16[1,2,192,1280]{3,1,0,2:T(2,128)(2,1)S(1)}, u32[]{:S(2)}, u32[]{:S(2)}) %all-to-all-start.1) | async-done | bytes 983072 | tf_op jit(solution)/shard_map/all_to_all | solution.py:88
  162.0 0.1 copy.33
  162.2 0.7 convolution_bitcast_fusion
  163.0 0.7 convolution_bitcast_fusion.1
  163.7 0.7 fusion
  164.4 2.2 %copy.29 = bf16[3,2,256,1280]{3,2,1,0:T(8,128)(2,1)} copy(bf16[3,2,256,1280]{3,2,0,1:T(8,128)(2,1)S(1)} %fusion) | data formatting | bytes 7864320 | tf_op jit(solution)/shard_map/convert_element_type | solution.py:56
  (34 shorter events, 0.9 us)
Async XLA Ops:
  6.5 11.2 %copy-start.2 = (s32[64]{0:T(128)S(1)}, s32[64]{0:T(128)}, u32[]{:S(2)}) copy-start(s32[64]{0:T(128)} %param.9) | copy-start | bytes 772
  6.5 103.0 %all-reduce.3.cloned.1.call-start = ((), (), s32[]{:S(2)}) async-start(), calls=%async_computation.2 | async-start | bytes 393216 | tf_op jit(solution)/shard_map/psum | solution.py:85
  7.7 17.8 %collective-permute-start = (bf16[1280,256]{1,0:T(8,128)(2,1)S(1)}, bf16[1280,256]{1,0:T(8,128)(2,1)S(1)}, u32[]{:S(2)}, u32[]{:S(2)}) collective-permute-start(bf16[1280,256]{1,0:T(8,128)(2,1)S(1)} %slice.109), channel_id=1, source_target_pairs={{0,4},{4,8},{8,12},{12,16},{16,20},{20,24},{24,28},{28,32},{32,36}... | collective-permute-start | bytes 1966088 | tf_op jit(solution)/shard_map/ppermute | solution.py:17
  22.2 4.7 %copy-start = (bf16[1280,4096]{1,0:T(8,128)(2,1)S(1)}, bf16[1280,4096]{1,0:T(8,128)(2,1)}, u32[]{:S(2)}) copy-start(bf16[1280,4096]{1,0:T(8,128)(2,1)} %param.5) | copy-start | bytes 31457284
  28.4 5.5 %copy-start.1 = (bf16[1280,8,768]{2,0,1:T(8,128)(2,1)}, bf16[1280,8,768]{2,0,1:T(8,128)(2,1)S(1)}, u32[]{:S(2)}) copy-start(bf16[1280,8,768]{2,0,1:T(8,128)(2,1)S(1)} %bitcast_dynamic-update-slice_fusion) | copy-start | bytes 47185924
  44.6 2.7 %copy-start.3 = (s32[256]{0:T(256)S(1)}, s32[256]{0:T(256)}, u32[]{:S(2)}) copy-start(s32[256]{0:T(256)} %param.8) | copy-start | bytes 3076
  111.4 18.0 %all-to-all-start = ((bf16[1,2,192,256]{3,1,0,2:T(2,128)(2,1)}), bf16[1,2,192,256]{3,1,0,2:T(2,128)(2,1)S(1)}, u32[]{:S(2)}, u32[]{:S(2)}) async-start(bf16[1,2,192,256]{3,1,0,2:T(2,128)(2,1)} %copy.25), calls=%async_computation | async-start | bytes 393216 | tf_op jit(solution)/shard_map/all_to_all | solution.py:86
  129.4 32.6 %all-to-all-start.1 = ((bf16[1,2,192,1280]{3,1,0,2:T(2,128)(2,1)}), bf16[1,2,192,1280]{3,1,0,2:T(2,128)(2,1)S(1)}, u32[]{:S(2)}, u32[]{:S(2)}) async-start(bf16[1,2,192,1280]{3,1,0,2:T(2,128)(2,1)} %copy.27), calls=%async_computation.1 | async-start | bytes 1966080 | tf_op jit(solution)/shard_map/all_to_all | solution.py:88
Sparse Core Ops, SparseCore 0:
  48.7 60.8 all-reduce.2
where the time goes:
time: 174 us; the launch traced here: 173 us
  waiting for transfers between devices  99.2 us (57%)
  local copies, waits for them, and re-layouts  19 us (11%)
  starting transfers between devices  17.8 us (10%)
  matrix products  15.5 us (9%)
  between operations  14.4 us (8%)
  other arithmetic  7.52 us (4%)
    psum x1, waiting for transfers between devices, per_device(): summed = lax.psum(picked[None].astype(jnp.bfloat16), 'chan')  61 us
    all_to_all x1, waiting for transfers between devices, per_device(): lax.all_to_all(white[None], 'seg', split_axis=2, concat_axis=0, tiled=True)  26.7 us
    dot_general x1, matrix products, per_device(): jnp.einsum('cbi,ij->cbj', windows, hmat, preferred_element_type=jnp.float32)  10.7 us
    all_to_all x1, waiting for transfers between devices, per_device(): lax.all_to_all(summed, 'seg', split_axis=2, concat_axis=0, tiled=True)  8.2 us
    all_to_all x1, starting transfers between devices, per_device(): lax.all_to_all(summed, 'seg', split_axis=2, concat_axis=0, tiled=True)  7.75 us
    unnamed x14, local copies, waits for them, and re-layouts  6.76 us
    all_to_all x1, starting transfers between devices, per_device(): lax.all_to_all(white[None], 'seg', split_axis=2, concat_axis=0, tiled=True)  5.65 us
    another operation x2, other arithmetic  4.67 us
  transfers between devices with their start and end apart: 4, of which 4 were waited for; matrix products, arithmetic and copies ran while one was open for 7% of the time, Pallas kernels for 0%

commit v1 on v0

v1 whole, which is shorter than its diff:
```python
import functools
import math

import jax
import jax.numpy as jnp
from jax import lax
from jax.experimental import pallas as pl
from jax.experimental.pallas import tpu as pltpu
from jax.sharding import PartitionSpec as P

NFFT = 1024
DEC = 4
TAPS = 256
BIN_DEV = 3
LANE = 128
BLOCK = 256
SPAN = DEC * BLOCK + TAPS
CHUNKS = ((0, 384), (384, 384), (768, 256), (1024, 256))
MAIN = (0, 1, 3, 4, 6, 7, 8, 9)
SPARE = ((2, 0), (2, 1), (2, 2), (5, 0), (5, 1), (5, 2), None, None)
MESH = pl.DeviceIdType.MESH


def fir_matrix(base_ref, hmat):
    rolled = pltpu.roll(
        jnp.broadcast_to(base_ref[...], (64, 512)), 0, 1, stride=DEC, stride_axis=0
    )
    rows = []
    for part in range(BLOCK // 64):
        pieces = []
        if part:
            pieces.append(jnp.zeros((64, 256 * part), jnp.float32))
        pieces.append(rolled)
        if part < 3:
            pieces.append(jnp.zeros((64, 256 * (3 - part)), jnp.float32))
        rows.append(jnp.concatenate(pieces, axis=1))
    hmat[...] = jnp.concatenate(rows, axis=0).T.astype(jnp.bfloat16)


def dft_table(band_ref, table, nseg):
    def block(i, _):
        row = i * 64 + lax.broadcasted_iota(jnp.int32, (64, LANE), 0)
        lane = lax.broadcasted_iota(jnp.int32, (64, LANE), 1)
        part = (row >> 2) & 1
        which = row & 3
        freq = band_ref[0] + BIN_DEV * (row >> 3) + which
        live = which < BIN_DEV

        def unit(turn):
            turn = turn & (NFFT - 1)
            quad = ((turn + 128) >> 8) & 3
            rest = ((turn + 128) & 255) - 128
            x = rest.astype(jnp.float32) * (2.0 * math.pi / NFFT)
            x2 = x * x
            sin = x * (1.0 + x2 * (-1.0 / 6 + x2 * (1.0 / 120 + x2 * (-1.0 / 5040 + x2 / 362880))))
            cos = 1.0 + x2 * (
                -0.5 + x2 * (1.0 / 24 + x2 * (-1.0 / 720 + x2 * (1.0 / 40320 - x2 / 3628800)))
            )
            swap = (quad & 1) == 1
            c = jnp.where(swap, sin, cos)
            s = jnp.where(swap, cos, sin)
            c = jnp.where((quad == 1) | (quad == 2), -c, c)
            s = jnp.where(quad >= 2, -s, s)
            return c, s

        c, s = unit(freq * lane + 256 * part)
        cr, sr = unit(freq * LANE)
        c = jnp.where(live, c, 0.0)
        s = jnp.where(live, s, 0.0)
        for a in range(NFFT // LANE):
            table[pl.ds(pl.multiple_of(i * 64, 64), 64), a * LANE : (a + 1) * LANE] = c.astype(
                jnp.bfloat16
            )
            c, s = c * cr - s * sr, s * cr + c * sr
        return 0

    lax.fori_loop(0, nseg // 8, block, 0)


def kernel(
    nseg,
    raw,
    base_ref,
    band_ref,
    src_ref,
    dead_ref,
    right_ref,
    left_ref,
    xbuf,
    tail,
    trace,
    first,
    hmat,
    table,
    halo_out,
    halo_in,
    spec,
    fill,
    outbox,
    inbox,
    wide,
    picked,
    half_in,
    half_sum,
    far_in,
    total,
    tail_sem,
    raw_sem,
    halo_send,
    halo_recv,
    box_send,
    box_recv,
    ex_send,
    ex_recv,
):
    seg = lax.axis_index("seg")
    chan = lax.axis_index("chan")
    chans = raw.shape[0]
    samples = raw.shape[1]
    core = chan & 1
    sibling = {"chan": chan ^ 1}
    far = {"chan": chan ^ 2}
    nextseg = {"seg": lax.rem(seg + 1, nseg)}

    tail_copy = pltpu.make_async_copy(raw.at[:, pl.ds(samples - TAPS, TAPS)], tail, tail_sem)
    tail_copy.start()
    raw_copies = [
        pltpu.make_async_copy(
            raw.at[pl.ds(i * BLOCK, BLOCK)], xbuf.at[pl.ds(i * BLOCK, BLOCK)], raw_sem.at[i]
        )
        for i in range(chans // BLOCK)
    ]
    for copy in raw_copies:
        copy.start()

    barrier = pltpu.get_barrier_semaphore()

    @pl.loop(1, nseg)
    def _(d):
        pl.semaphore_signal(
            barrier, 1, device_id={"seg": lax.rem(seg + d, nseg)}, device_id_type=MESH
        )

    pl.semaphore_signal(barrier, 1, device_id=sibling, device_id_type=MESH)
    pl.semaphore_signal(barrier, 1, device_id=far, device_id_type=MESH)

    fir_matrix(base_ref, hmat)
    tail_copy.wait()
    lane64 = lax.broadcasted_iota(jnp.int32, (1, LANE), 1) < 64
    near = hmat[0:TAPS, 0:LANE]
    near = jnp.where(lane64, near.astype(jnp.float32), 0.0)
    low = near.astype(jnp.bfloat16)
    high = pltpu.roll(near, 64, 1).astype(jnp.bfloat16)
    for c0, w in CHUNKS:
        h = w // 2
        part = jnp.dot(tail[c0 : c0 + h], low, preferred_element_type=jnp.float32) + jnp.dot(
            tail[c0 + h : c0 + w], high, preferred_element_type=jnp.float32
        )
        halo_out[c0 // 2 : c0 // 2 + h] = part.astype(jnp.bfloat16)

    dft_table(band_ref, table, nseg)
    pl.semaphore_wait(barrier, nseg + 1)
    halos = []
    for q, (c0, w) in enumerate(CHUNKS):
        rows = pl.ds(c0 // 2, w // 2)
        copy = pltpu.make_async_remote_copy(
            halo_out.at[rows],
            halo_in.at[rows],
            halo_send.at[q],
            halo_recv.at[q],
            device_id=nextseg,
            device_id_type=MESH,
        )
        copy.start()
        halos.append(copy)

    chan_row = chan * chans + lax.broadcasted_iota(jnp.int32, (1, chans), 1)

    def mark(i, hit):
        return jnp.where(chan_row == dead_ref[i], 0.0, hit)

    alive = lax.fori_loop(0, dead_ref.shape[0], mark, jnp.ones((1, chans), jnp.float32))

    for i in range(chans // BLOCK):
        rows = slice(i * BLOCK, (i + 1) * BLOCK)
        raw_copies[i].wait()
        for b in range(NFFT // BLOCK):
            begin = b * DEC * BLOCK - TAPS
            if b == 0:
                acc = jnp.dot(
                    xbuf[rows, 0 : DEC * BLOCK], hmat[TAPS:], preferred_element_type=jnp.float32
                )
                first[rows] = acc[:, :LANE]
                trace[rows, LANE:BLOCK] = acc[:, LANE:].astype(jnp.bfloat16)
            else:
                acc = jnp.dot(
                    xbuf[rows, begin : begin + SPAN], hmat[...], preferred_element_type=jnp.float32
                )
                trace[rows, b * BLOCK : (b + 1) * BLOCK] = acc.astype(jnp.bfloat16)

    has_prior = jnp.where(seg > 0, 1.0, 0.0)
    spare_row = (lax.broadcasted_iota(jnp.int32, (1, 8, 1), 1) & 3) == 3
    for q, (c0, w) in enumerate(CHUNKS):
        h = w // 2
        halos[q].wait_recv()
        prior = halo_in[c0 // 2 : c0 // 2 + h].astype(jnp.float32) * has_prior
        prior_low = jnp.where(lane64, prior, 0.0)
        prior_high = jnp.where(lane64, pltpu.roll(prior, 64, 1), 0.0)
        trace[c0 : c0 + h, 0:LANE] = (first[c0 : c0 + h] + prior_low).astype(jnp.bfloat16)
        trace[c0 + h : c0 + w, 0:LANE] = (first[c0 + h : c0 + w] + prior_high).astype(jnp.bfloat16)
        spec[:, :w] = lax.dot_general(
            table[...],
            trace[c0 : c0 + w],
            (((1,), (1,)), ((), ())),
            preferred_element_type=jnp.float32,
        )

        def square(i, acc, w=w):
            s = spec[pl.ds(pl.multiple_of(i * 64, 64), 64), :w].reshape(8, 8, w)
            return acc + jnp.sum(s * s, axis=0)

        energy = lax.fori_loop(0, nseg // 8, square, jnp.zeros((8, w), jnp.float32))
        level = jnp.sum(energy, axis=0, keepdims=True) * (1.0 / (BIN_DEV * nseg))
        floor = (0.1 * level + 1e-6).reshape(1, 1, w)
        live = alive[:, c0 : c0 + w].reshape(1, 1, w)

        def white(i, _, w=w, q=q, floor=floor, live=live):
            dest = pl.ds(i * 8, 8)
            s = spec[pl.ds(pl.multiple_of(i * 64, 64), 64), :w].reshape(8, 8, w)
            sq = s * s
            power = sq + pltpu.roll(sq, 4, 1)
            out = s * (live * lax.rsqrt(power + floor))
            one = out[:, :, 0:LANE]
            two = out[:, :, LANE : 2 * LANE]
            if q == 0:
                extra = out[:, :, 2 * LANE :]
                one = jnp.where(spare_row, pltpu.roll(extra, 3, 1), one)
                two = jnp.where(spare_row, pltpu.roll(extra, 2, 1), two)
                fill[0, dest] = pltpu.roll(extra, 1, 1)
            elif q == 1:
                extra = out[:, :, 2 * LANE :]
                one = jnp.where(spare_row, fill[0, dest], one)
                two = jnp.where(spare_row, pltpu.roll(extra, 3, 1), two)
                fill[1, dest] = pltpu.roll(extra, 2, 1)
                fill[2, dest] = pltpu.roll(extra, 1, 1)
            elif q == 2:
                one = jnp.where(spare_row, fill[1, dest], one)
                two = jnp.where(spare_row, fill[2, dest], two)
            outbox[q, dest] = jnp.concatenate([one, two], axis=1).astype(jnp.bfloat16)
            return 0

        lax.fori_loop(0, nseg // 8, white, 0)

        pltpu.make_async_copy(outbox.at[q, seg], inbox.at[q, seg], box_recv.at[q]).start()

        @pl.loop(1, nseg)
        def _(d, q=q):
            to = lax.rem(seg + d, nseg)
            pltpu.make_async_remote_copy(
                outbox.at[q, to],
                inbox.at[q, seg],
                box_send.at[q],
                box_recv.at[q],
                device_id={"seg": to},
                device_id_type=MESH,
            ).start()

    for q in range(len(CHUNKS)):
        pltpu.make_async_copy(inbox.at[q], inbox.at[q], box_recv.at[q]).wait()
        wide[...] = inbox[q].reshape(nseg * 16, LANE).astype(jnp.float32)
        for slab in range(2):
            at = 2 * q + slab
            for i in range(8):
                part, which = i // 4, i % 4
                group = MAIN[at]
                if which == 3:
                    if SPARE[at] is None:
                        continue
                    group, which = SPARE[at]
                rows = wide[pl.ds(slab * 8 + i, nseg, stride=16), :]
                right_ref[
                    which, part * nseg : (part + 1) * nseg, group * LANE : (group + 1) * LANE
                ] = rows.astype(jnp.bfloat16)

    here = chan * chans
    for b in range(BIN_DEV):
        acc = jnp.zeros((2 * nseg, src_ref.shape[1]), jnp.float32)
        for c0 in range(0, chans, BLOCK):
            ids = here + c0 + lax.broadcasted_iota(jnp.int32, (BLOCK, src_ref.shape[1]), 0)
            hot = jnp.where(ids == src_ref[...], 1.0, 0.0).astype(jnp.bfloat16)
            acc += jnp.dot(
                right_ref[b, :, c0 : c0 + BLOCK], hot, preferred_element_type=jnp.float32
            )
        acc = acc.astype(jnp.bfloat16)
        picked[b, 0] = acc[:nseg]
        picked[b, 1] = acc[nseg:]

    def exchange(step, b, src, dst, to):
        copy = pltpu.make_async_remote_copy(
            src,
            dst,
            ex_send.at[step, b],
            ex_recv.at[step, b],
            device_id=to,
            device_id_type=MESH,
        )
        copy.start()
        return copy

    other = 1 - core
    steps = [[exchange(0, b, picked.at[b, other], half_in.at[b], sibling) for b in range(BIN_DEV)]]
    steps.append([])
    for b in range(BIN_DEV):
        steps[0][b].wait_recv()
        half_sum[b] = picked[b, core] + half_in[b]
        steps[1].append(exchange(1, b, half_sum.at[b], far_in.at[b], far))
    steps.append([])
    for b in range(BIN_DEV):
        steps[1][b].wait_recv()
        total[b, core] = half_sum[b] + far_in[b]
        steps[2].append(exchange(2, b, total.at[b, core], total.at[b, core], sibling))
    for b in range(BIN_DEV):
        steps[2][b].wait_recv()
        left_ref[b, :nseg] = total[b, 0]
        left_ref[b, nseg:] = total[b, 1]
    for step in steps:
        for copy in step:
            copy.wait_send()
    for copy in halos:
        copy.wait_send()
    for q in range(len(CHUNKS)):
        sent = outbox.at[q, pl.ds(0, nseg - 1)]
        pltpu.make_async_copy(sent, sent, box_send.at[q]).wait()


def correlate_kernel(factor, left_ref, right_ref, out_ref):
    half = left_ref.shape[1] // 2
    right = right_ref[0]
    left = left_ref[0] * jnp.bfloat16(factor)
    turned = jnp.concatenate([-left[half:], left[:half]], axis=0)
    for part, lhs in enumerate((left, turned)):
        out_ref[0, part] = lax.dot_general(
            lhs, right, (((0,), (0,)), ((), ())), preferred_element_type=jnp.float32
        ).astype(jnp.bfloat16)


def per_device(nseg, raw, fir_taps, band_lo, source_chan, dead_chan):
    chans = raw.shape[0]
    nsrc = source_chan.shape[0]
    base = jnp.pad(fir_taps[::-1].astype(jnp.float32), (DEC, 512 - TAPS - DEC)).reshape(1, 512)
    vmem = pl.BlockSpec(memory_space=pltpu.VMEM)
    smem = pl.BlockSpec(memory_space=pltpu.SMEM)
    bf16, f32 = jnp.bfloat16, jnp.float32
    nq = len(CHUNKS)
    right, left = pl.pallas_call(
        functools.partial(kernel, nseg),
        out_shape=(
            jax.ShapeDtypeStruct((BIN_DEV, 2 * nseg, chans), bf16),
            jax.ShapeDtypeStruct((BIN_DEV, 2 * nseg, nsrc), bf16),
        ),
        in_specs=[pl.BlockSpec(memory_space=pl.ANY), vmem, smem, vmem, smem],
        out_specs=(vmem, vmem),
        scratch_shapes=[
            pltpu.VMEM(raw.shape, bf16),
            pltpu.VMEM((chans, TAPS), bf16),
            pltpu.VMEM((chans, NFFT), bf16),
            pltpu.VMEM((chans, LANE), f32),
            pltpu.VMEM((SPAN, BLOCK), bf16),
            pltpu.VMEM((8 * nseg, NFFT), bf16),
            pltpu.VMEM((chans // 2, LANE), bf16),
            pltpu.VMEM((chans // 2, LANE), bf16),
            pltpu.VMEM((8 * nseg, 384), f32),
            pltpu.VMEM((3, nseg, 8, LANE), f32),
            pltpu.VMEM((nq, nseg, 16, LANE), bf16),
            pltpu.VMEM((nq, nseg, 16, LANE), bf16),
            pltpu.VMEM((nseg * 16, LANE), f32),
            pltpu.VMEM((BIN_DEV, 2, nseg, nsrc), bf16),
            pltpu.VMEM((BIN_DEV, nseg, nsrc), bf16),
            pltpu.VMEM((BIN_DEV, nseg, nsrc), bf16),
            pltpu.VMEM((BIN_DEV, nseg, nsrc), bf16),
            pltpu.VMEM((BIN_DEV, 2, nseg, nsrc), bf16),
            pltpu.SemaphoreType.DMA,
            pltpu.SemaphoreType.DMA((chans // BLOCK,)),
            pltpu.SemaphoreType.DMA((nq,)),
            pltpu.SemaphoreType.DMA((nq,)),
            pltpu.SemaphoreType.DMA((nq,)),
            pltpu.SemaphoreType.DMA((nq,)),
            pltpu.SemaphoreType.DMA((3, BIN_DEV)),
            pltpu.SemaphoreType.DMA((3, BIN_DEV)),
        ],
        compiler_params=pltpu.CompilerParams(
            collective_id=0, has_side_effects=True, vmem_limit_bytes=48 * 1024 * 1024
        ),
        name="whiten_exchange",
    )(raw, base, band_lo, source_chan.reshape(1, nsrc), dead_chan)
    return pl.pallas_call(
        functools.partial(correlate_kernel, 1.0 / math.sqrt(nseg)),
        grid=(BIN_DEV,),
        out_shape=jax.ShapeDtypeStruct((BIN_DEV, 2, nsrc, chans), bf16),
        in_specs=[
            pl.BlockSpec((1, 2 * nseg, nsrc), lambda b: (b, 0, 0)),
            pl.BlockSpec((1, 2 * nseg, chans), lambda b: (b, 0, 0)),
        ],
        out_specs=pl.BlockSpec((1, 2, nsrc, chans), lambda b: (b, 0, 0, 0)),
        compiler_params=pltpu.CompilerParams(vmem_limit_bytes=32 * 1024 * 1024),
        name="correlate",
    )(left, right)


def solution(mesh):
    return jax.shard_map(
        functools.partial(per_device, mesh.shape["seg"]),
        mesh=mesh,
        in_specs=(P("chan", "seg"), P(), P(), P(), P()),
        out_specs=P("seg", None, None, "chan"),
        check_vma=False,
    )
```

time: 174 us -> 61.7 us (0.35)
  waiting for transfers between devices: 99.2 us -> 0 us
  Pallas kernels: 0 us -> 58.8 us
  starting transfers between devices: 17.8 us -> 0 us
  local copies, waits for them, and re-layouts: 19 us -> 2.08 us
  matrix products: 15.5 us -> 0 us
  between operations: 14.4 us -> 0.66 us
  other arithmetic: 7.52 us -> 0.08 us
    psum x1 -> x0, waiting for transfers between devices: 61 us -> none  [per_device(): summed = lax.psum(picked[None].astype(jnp.bfloat16), 'chan')]
    pallas_call x0 -> x2, Pallas kernels: none -> 58.8 us  [the longest x1 55.6 us: per_device(): pl.pallas_call(functools.partial(kernel, nseg), out_shape=(jax.ShapeDtype...]
    all_to_all x2 -> x0, waiting for transfers between devices: 34.9 us -> none  [the longest x1 26.7 us: per_device(): lax.all_to_all(white[None], 'seg', split_axis=2, concat_axis=0, tiled=True)]
    dot_general x5 -> x0, matrix products: 15.5 us -> none  [the longest x1 10.7 us: per_device(): jnp.einsum('cbi,ij->cbj', windows, hmat, preferred_element_type=jnp.float32)]
    all_to_all x2 -> x0, starting transfers between devices: 13.4 us -> none  [the longest x1 7.75 us: per_device(): lax.all_to_all(summed, 'seg', split_axis=2, concat_axis=0, tiled=True)]
    unnamed x14 -> x4, local copies, waits for them, and re-layouts: 6.76 us -> 1.33 us
    another operation x4 -> x0, other arithmetic: 4.79 us -> none
    ppermute x1 -> x0, starting transfers between devices: 4.41 us -> none  [shifted(): return lax.ppermute(block, axis, route)]
  transfers between devices with their start and end apart: 4 -> 0, of which waited for: 4 -> 0; matrix products, arithmetic and copies ran while one was open for 7% -> 0% of each run, Pallas kernels for 0% -> 0%
where the time goes in v1:
time: 61.7 us; the launch traced here: 61.6 us
  Pallas kernels  58.8 us (95%)
  local copies, waits for them, and re-layouts  2.08 us (3%)
  between operations  0.66 us (1%)
    pallas_call x1, Pallas kernels, per_device(): pl.pallas_call(functools.partial(kernel, nseg), out_shape=(jax.ShapeDtype...  55.6 us
    pallas_call x1, Pallas kernels, per_device(): pl.pallas_call(functools.partial(correlate_kernel, 1.0 / math.sqrt(nseg))...  3.2 us
    unnamed x4, local copies, waits for them, and re-layouts  1.33 us

profile of v1, /device:TPU:1, one launch (start us, length us, event | category | flops | bytes accessed | tf_op | source)
XLA Modules:
  0.0 61.6 jit_solution(11158178683083318235)
XLA Ops:
  0.7 0.7 %rev.3 = bf16[256]{0:T(256)(128)(2,1)S(1)} reverse(bf16[256]{0:T(256)(128)(2,1)} %param.6), dimensions={0} | reverse | bytes 1024 | tf_op jit(solution)/shard_map/rev | solution.py:350
  1.4 0.1 pad_convert_fusion
  1.5 0.0 copy-start
  1.5 0.7 %copy-done = s32[256]{0:T(256)S(1)} copy-done((s32[256]{0:T(256)S(1)}, s32[256]{0:T(256)}, u32[]{:S(2)}) %copy-start) | copy-done | bytes 1048
  2.2 0.0 copy-start.1
  2.2 0.7 %copy-done.1 = s32[64]{0:T(128)S(1)} copy-done((s32[64]{0:T(128)S(1)}, s32[64]{0:T(128)}, u32[]{:S(2)}) %copy-start.1) | copy-done | bytes 280
  2.8 55.6 %whiten_exchange.1 = (bf16[3,128,1280]{2,1,0:T(8,128)(2,1)S(1)}, bf16[3,128,256]{2,1,0:T(8,128)(2,1)S(1)}) custom-call(bf16[1280,4096]{1,0:T(8,128)(2,1)} %raw.1, f32[1,512]{1,0:T(1,128)S(1)} %bitcast.2, s32[1]{0:T(128)S(6)} %copy.6.band_ref, s32[1,256]{1,0:T(1,128)S(1)} %bitcast.3, s32[64]{0:T(128)S(1)} %copy-done.1), custom_call_target="tpu_custom_call" | custom-call | tf_op jit(solution)/shard_map/whiten_exchange/pallas_call | solution.py:355
  58.4 3.2 %correlate.1 = bf16[3,2,256,1280]{3,2,1,0:T(8,128)(2,1)} custom-call(bf16[3,128,256]{2,1,0:T(8,128)(2,1)S(1)} %get-tuple-element.7.left_ref, bf16[3,128,1280]{2,1,0:T(8,128)(2,1)S(1)} %get-tuple-element.8.right_ref), custom_call_target="tpu_custom_call" | custom-call | tf_op jit(solution)/shard_map/correlate/pallas_call | solution.py:396
Async XLA Ops:
  1.5 0.7 %copy-start = (s32[256]{0:T(256)S(1)}, s32[256]{0:T(256)}, u32[]{:S(2)}) copy-start(s32[256]{0:T(256)} %param.8) | copy-start | bytes 3076
  2.2 0.7 %copy-start.1 = (s32[64]{0:T(128)S(1)}, s32[64]{0:T(128)}, u32[]{:S(2)}) copy-start(s32[64]{0:T(128)} %dead_ref.1) | copy-start | bytes 772

commit v2 on v1

v2 whole, which is shorter than its diff:
```python
import functools
import math

import jax
import jax.numpy as jnp
from jax import lax
from jax.experimental import pallas as pl
from jax.experimental.pallas import tpu as pltpu
from jax.sharding import PartitionSpec as P

NFFT = 1024
DEC = 4
TAPS = 256
BINS = 3
LANE = 128
BLOCK = 256
SPAN = DEC * BLOCK + TAPS
CHUNKS = ((1024, 256), (0, 512), (512, 512))
ROWS = 16
MESH = pl.DeviceIdType.MESH


def box_row(part, b, group):
    if group < 8:
        return 1 + b, 8 * part + group
    return 0, 8 * part + 2 * b + group - 8


def fir_rows(taps):
    tap_no = lax.broadcasted_iota(jnp.int32, (TAPS, 512), 0)
    place = lax.broadcasted_iota(jnp.int32, (TAPS, 512), 1)
    onehot = jnp.where(tap_no + place == TAPS + DEC - 1, 1.0, 0.0).astype(jnp.bfloat16)
    base = jnp.dot(
        jnp.broadcast_to(taps, (64, TAPS)).astype(jnp.bfloat16),
        onehot,
        preferred_element_type=jnp.float32,
    )
    return pltpu.roll(base, 0, 1, stride=DEC, stride_axis=0)


def fir_matrix(rolled):
    rows = []
    for part in range(BLOCK // 64):
        pieces = []
        if part:
            pieces.append(jnp.zeros((64, 256 * part), jnp.float32))
        pieces.append(rolled)
        if part < 3:
            pieces.append(jnp.zeros((64, 256 * (3 - part)), jnp.float32))
        rows.append(jnp.concatenate(pieces, axis=1))
    return jnp.concatenate(rows, axis=0).T.astype(jnp.bfloat16)


def dft_table(band_ref, table, nseg):
    def block(i, _):
        part = i // BINS
        freq = band_ref[0] + i % BINS + BINS * lax.broadcasted_iota(jnp.int32, (nseg, LANE), 0)
        lane = lax.broadcasted_iota(jnp.int32, (nseg, LANE), 1)

        def unit(turn):
            turn = turn & (NFFT - 1)
            quad = ((turn + 128) >> 8) & 3
            rest = ((turn + 128) & 255) - 128
            x = rest.astype(jnp.float32) * (2.0 * math.pi / NFFT)
            x2 = x * x
            sin = x * (1.0 + x2 * (-1.0 / 6 + x2 * (1.0 / 120 + x2 * (-1.0 / 5040 + x2 / 362880))))
            cos = 1.0 + x2 * (
                -0.5 + x2 * (1.0 / 24 + x2 * (-1.0 / 720 + x2 * (1.0 / 40320 - x2 / 3628800)))
            )
            swap = (quad & 1) == 1
            c = jnp.where(swap, sin, cos)
            s = jnp.where(swap, cos, sin)
            c = jnp.where((quad == 1) | (quad == 2), -c, c)
            s = jnp.where(quad >= 2, -s, s)
            return c, s

        c, s = unit(freq * lane + 256 * part)
        cr, sr = unit(freq * LANE)
        for a in range(NFFT // LANE):
            rows = pl.ds(pl.multiple_of(i * nseg, nseg), nseg)
            table[rows, a * LANE : (a + 1) * LANE] = c.astype(jnp.bfloat16)
            c, s = c * cr - s * sr, s * cr + c * sr
        return 0

    lax.fori_loop(0, 2 * BINS, block, 0)


def products(left, right, factor):
    half = left.shape[0] // 2
    left = left * jnp.bfloat16(factor)
    turned = jnp.concatenate([-left[half:], left[:half]], axis=0)
    return [
        lax.dot_general(
            lhs, right, (((0,), (0,)), ((), ())), preferred_element_type=jnp.float32
        ).astype(jnp.bfloat16)
        for lhs in (left, turned)
    ]


def kernel(
    nseg,
    factor,
    nsrc,
    ndead,
    raw,
    small_ref,
    band_ref,
    done_ref,
    right_last,
    left_last,
    hot,
    xbuf,
    tail,
    trace,
    first,
    hmat,
    table,
    halo_out,
    halo_in,
    spec,
    tiles,
    outbox,
    inbox,
    wide,
    right_ref,
    picked,
    half_in,
    half_sum,
    far_in,
    total,
    tail_sem,
    raw_sem,
    halo_send,
    halo_recv,
    box_send,
    box_recv,
    ex_send,
    ex_recv,
):
    seg = lax.axis_index("seg")
    chan = lax.axis_index("chan")
    chans = raw.shape[0]
    samples = raw.shape[1]
    core = chan & 1
    sibling = {"chan": chan ^ 1}
    far = {"chan": chan ^ 2}
    nextseg = {"seg": lax.rem(seg + 1, nseg)}

    tail_copy = pltpu.make_async_copy(raw.at[:, pl.ds(samples - TAPS, TAPS)], tail, tail_sem)
    raw_copies = [
        pltpu.make_async_copy(raw.at[pl.ds(c0, w)], xbuf.at[pl.ds(c0, w)], raw_sem.at[q])
        for q, (c0, w) in enumerate(CHUNKS)
    ]
    for copy in (tail_copy, raw_copies[0], raw_copies[1]):
        copy.start()

    barrier = pltpu.get_barrier_semaphore()

    @pl.loop(1, nseg)
    def _(d):
        pl.semaphore_signal(
            barrier, 1, device_id={"seg": lax.rem(seg + d, nseg)}, device_id_type=MESH
        )

    pl.semaphore_signal(barrier, 1, device_id=sibling, device_id_type=MESH)
    pl.semaphore_signal(barrier, 1, device_id=far, device_id_type=MESH)

    rolled = fir_rows(small_ref[:, :TAPS])
    lane64 = lax.broadcasted_iota(jnp.int32, (1, LANE), 1) < 64
    near = rolled[:, :TAPS]
    low = jnp.concatenate([near, jnp.zeros_like(near)], axis=0).astype(jnp.bfloat16)
    high = jnp.concatenate([jnp.zeros_like(near), near], axis=0).astype(jnp.bfloat16)
    over_time = (((1,), (1,)), ((), ()))
    tail_copy.wait()
    for c0, w in CHUNKS:
        h = w // 2
        part = lax.dot_general(
            tail[c0 : c0 + h], low, over_time, preferred_element_type=jnp.float32
        ) + lax.dot_general(
            tail[c0 + h : c0 + w], high, over_time, preferred_element_type=jnp.float32
        )
        halo_out[c0 // 2 : c0 // 2 + h] = part.astype(jnp.bfloat16)

    pl.semaphore_wait(barrier, nseg + 1)
    halos = []
    for q, (c0, w) in enumerate(CHUNKS):
        rows = pl.ds(c0 // 2, w // 2)
        copy = pltpu.make_async_remote_copy(
            halo_out.at[rows],
            halo_in.at[rows],
            halo_send.at[q],
            halo_recv.at[q],
            device_id=nextseg,
            device_id_type=MESH,
        )
        copy.start()
        halos.append(copy)

    hmat[...] = fir_matrix(rolled)

    def filtered(q):
        c0, w = CHUNKS[q]
        rows = slice(c0, c0 + w)
        raw_copies[q].wait()
        if q + 2 < len(CHUNKS):
            raw_copies[q + 2].start()
        for b in range(NFFT // BLOCK):
            begin = b * DEC * BLOCK - TAPS
            if b == 0:
                acc = jnp.dot(
                    xbuf[rows, 0 : DEC * BLOCK], hmat[TAPS:], preferred_element_type=jnp.float32
                )
                first[rows] = acc[:, :LANE]
                trace[rows, LANE:BLOCK] = acc[:, LANE:].astype(jnp.bfloat16)
            else:
                acc = jnp.dot(
                    xbuf[rows, begin : begin + SPAN], hmat[...], preferred_element_type=jnp.float32
                )
                trace[rows, b * BLOCK : (b + 1) * BLOCK] = acc.astype(jnp.bfloat16)

    filtered(0)
    dft_table(band_ref, table, nseg)

    first_chan = (chan * chans).astype(jnp.float32)
    padded = small_ref[:, TAPS + nsrc :]
    dead = jnp.broadcast_to(padded, (LANE, LANE)).T[:ndead]
    lane = lax.broadcasted_iota(jnp.int32, (1, LANE), 1).astype(jnp.float32)
    alive = []
    for c0 in range(0, chans, LANE):
        hits = jnp.where(dead == lane + (first_chan + c0), 1.0, 0.0)
        alive.append(1.0 - jnp.max(hits, axis=0, keepdims=True))
    has_prior = jnp.where(seg > 0, 1.0, 0.0)
    nothing = jnp.zeros((nseg, LANE), jnp.float32)
    for row in (6, 7, 14, 15):
        tiles[0, pl.ds(row, nseg, stride=ROWS), :] = nothing

    def post(box):
        outbox[box] = tiles[box].reshape(nseg, ROWS, LANE).astype(jnp.bfloat16)
        pltpu.make_async_copy(outbox.at[box, seg], inbox.at[box, seg], box_recv.at[box]).start()

        @pl.loop(1, nseg)
        def _(d):
            to = lax.rem(seg + d, nseg)
            pltpu.make_async_remote_copy(
                outbox.at[box, to],
                inbox.at[box, seg],
                box_send.at[box],
                box_recv.at[box],
                device_id={"seg": to},
                device_id_type=MESH,
            ).start()

    for q, (c0, w) in enumerate(CHUNKS):
        h = w // 2
        halos[q].wait_recv()
        prior = halo_in[c0 // 2 : c0 // 2 + h].astype(jnp.float32) * has_prior
        prior_low = jnp.where(lane64, prior, 0.0)
        prior_high = jnp.where(lane64, pltpu.roll(prior, 64, 1), 0.0)
        trace[c0 : c0 + h, 0:LANE] = (first[c0 : c0 + h] + prior_low).astype(jnp.bfloat16)
        trace[c0 + h : c0 + w, 0:LANE] = (first[c0 + h : c0 + w] + prior_high).astype(jnp.bfloat16)
        spec[:, :w] = lax.dot_general(
            table[...], trace[c0 : c0 + w], over_time, preferred_element_type=jnp.float32
        )
        for at in range(0, w, LANE):
            lanes = slice(at, at + LANE)
            group = (c0 + at) // LANE
            energy = jnp.zeros((8, LANE), jnp.float32)
            for row in range(2 * BINS):
                s = spec[row * nseg : (row + 1) * nseg, lanes].reshape(nseg // 8, 8, LANE)
                energy += jnp.sum(s * s, axis=0)
            level = jnp.sum(energy, axis=0, keepdims=True) * (1.0 / (BINS * nseg))
            live = alive[group]
            for b in range(BINS):
                real = spec[b * nseg : (b + 1) * nseg, lanes]
                imag = spec[(BINS + b) * nseg : (BINS + b + 1) * nseg, lanes]
                gain = live * lax.rsqrt(real * real + imag * imag + (0.1 * level + 1e-6))
                for part, value in enumerate((real, imag)):
                    box, row = box_row(part, b, group)
                    tiles[box, pl.ds(row, nseg, stride=ROWS), :] = value * gain
        if q == 0:
            post(0)
            filtered(1)
        elif q == 1:
            filtered(2)
    for b in range(BINS):
        post(1 + b)

    source = small_ref[:, TAPS : TAPS + nsrc]
    for c0 in range(0, chans, LANE):
        ids = lax.broadcasted_iota(jnp.int32, (LANE, nsrc), 0).astype(jnp.float32)
        hot[c0 : c0 + LANE] = jnp.where(ids + (first_chan + c0) == source, 1.0, 0.0).astype(
            jnp.bfloat16
        )

    def right_of(b):
        return right_last if b == BINS - 1 else right_ref.at[b]

    def collect(box):
        pltpu.make_async_copy(inbox.at[box], inbox.at[box], box_recv.at[box]).wait()
        wide[...] = inbox[box].reshape(nseg * ROWS, LANE).astype(jnp.float32)
        for part in range(2):
            for b in range(BINS):
                for group in range(chans // LANE):
                    held, row = box_row(part, b, group)
                    if held == box:
                        right_of(b)[
                            part * nseg : (part + 1) * nseg, group * LANE : (group + 1) * LANE
                        ] = wide[pl.ds(row, nseg, stride=ROWS), :].astype(jnp.bfloat16)

    copies = {}

    def exchange(step, b, src, dst, to):
        copy = pltpu.make_async_remote_copy(
            src,
            dst,
            ex_send.at[step, b],
            ex_recv.at[step, b],
            device_id=to,
            device_id_type=MESH,
        )
        copy.start()
        copies[step, b] = copy

    def step_pick(b):
        acc = jnp.dot(right_of(b)[...], hot[...], preferred_element_type=jnp.float32)
        acc = acc.astype(jnp.bfloat16)
        picked[b, 0] = acc[:nseg]
        picked[b, 1] = acc[nseg:]
        exchange(0, b, picked.at[b, 1 - core], half_in.at[b], sibling)

    def step_far(b):
        copies[0, b].wait_recv()
        half_sum[b] = picked[b, core] + half_in[b]
        exchange(1, b, half_sum.at[b], far_in.at[b], far)

    def step_back(b):
        copies[1, b].wait_recv()
        total[b, core] = half_sum[b] + far_in[b]
        exchange(2, b, total.at[b, core], total.at[b, core], sibling)

    def step_product(b):
        copies[2, b].wait_recv()
        left = jnp.concatenate([total[b, 0], total[b, 1]], axis=0)
        if b == BINS - 1:
            left_last[...] = left
            return
        for part, value in enumerate(products(left, right_ref[b], factor)):
            done_ref[b, part] = value

    collect(0)
    collect(1)
    step_pick(0)
    collect(2)
    step_pick(1)
    step_far(0)
    collect(3)
    step_pick(2)
    step_far(1)
    step_far(2)
    for b in range(BINS):
        step_back(b)
    for b in range(BINS):
        step_product(b)
    for copy in copies.values():
        copy.wait_send()
    for copy in halos:
        copy.wait_send()
    for box in range(outbox.shape[0]):
        sent = outbox.at[box, pl.ds(0, nseg - 1)]
        pltpu.make_async_copy(sent, sent, box_send.at[box]).wait()


def finish_kernel(factor, done_ref, right_ref, left_ref, out_ref, buf, sems):
    last = BINS - 1
    copies = [pltpu.make_async_copy(done_ref, out_ref.at[pl.ds(0, last)], sems.at[2])]
    copies[0].start()
    for part, value in enumerate(products(left_ref[...], right_ref[...], factor)):
        buf[part] = value
        copy = pltpu.make_async_copy(buf.at[part], out_ref.at[last, part], sems.at[part])
        copy.start()
        copies.append(copy)
    for copy in copies:
        copy.wait()


def per_device(nseg, raw, fir_taps, band_lo, source_chan, dead_chan):
    chans = raw.shape[0]
    nsrc = source_chan.shape[0]
    ndead = dead_chan.shape[0]
    factor = 1.0 / math.sqrt(nseg)
    vmem = pl.BlockSpec(memory_space=pltpu.VMEM)
    smem = pl.BlockSpec(memory_space=pltpu.SMEM)
    hbm = pl.BlockSpec(memory_space=pltpu.HBM)
    bf16, f32 = jnp.bfloat16, jnp.float32
    small = jnp.concatenate(
        [x.astype(f32) for x in (fir_taps, source_chan, dead_chan)]
        + [jnp.full((LANE - ndead,), -1.0, f32)]
    ).reshape(1, TAPS + nsrc + LANE)
    nq = len(CHUNKS)
    nbox = 1 + BINS
    done, right, left = pl.pallas_call(
        functools.partial(kernel, nseg, factor, nsrc, ndead),
        out_shape=(
            jax.ShapeDtypeStruct((BINS - 1, 2, nsrc, chans), bf16),
            jax.ShapeDtypeStruct((2 * nseg, chans), bf16),
            jax.ShapeDtypeStruct((2 * nseg, nsrc), bf16),
        ),
        in_specs=[hbm, vmem, smem],
        out_specs=(vmem, vmem, vmem),
        scratch_shapes=[
            pltpu.VMEM((chans, nsrc), bf16),
            pltpu.VMEM(raw.shape, bf16),
            pltpu.VMEM((chans, TAPS), bf16),
            pltpu.VMEM((chans, NFFT), bf16),
            pltpu.VMEM((chans, LANE), f32),
            pltpu.VMEM((SPAN, BLOCK), bf16),
            pltpu.VMEM((2 * BINS * nseg, NFFT), bf16),
            pltpu.VMEM((chans // 2, LANE), bf16),
            pltpu.VMEM((chans // 2, LANE), bf16),
            pltpu.VMEM((2 * BINS * nseg, 512), f32),
            pltpu.VMEM((nbox, nseg * ROWS, LANE), f32),
            pltpu.VMEM((nbox, nseg, ROWS, LANE), bf16),
            pltpu.VMEM((nbox, nseg, ROWS, LANE), bf16),
            pltpu.VMEM((nseg * ROWS, LANE), f32),
            pltpu.VMEM((BINS - 1, 2 * nseg, chans), bf16),
            pltpu.VMEM((BINS, 2, nseg, nsrc), bf16),
            pltpu.VMEM((BINS, nseg, nsrc), bf16),
            pltpu.VMEM((BINS, nseg, nsrc), bf16),
            pltpu.VMEM((BINS, nseg, nsrc), bf16),
            pltpu.VMEM((BINS, 2, nseg, nsrc), bf16),
            pltpu.SemaphoreType.DMA,
            pltpu.SemaphoreType.DMA((nq,)),
            pltpu.SemaphoreType.DMA((nq,)),
            pltpu.SemaphoreType.DMA((nq,)),
            pltpu.SemaphoreType.DMA((nbox,)),
            pltpu.SemaphoreType.DMA((nbox,)),
            pltpu.SemaphoreType.DMA((3, BINS)),
            pltpu.SemaphoreType.DMA((3, BINS)),
        ],
        compiler_params=pltpu.CompilerParams(
            collective_id=0, has_side_effects=True, vmem_limit_bytes=44 * 1024 * 1024
        ),
        name="whiten_exchange",
    )(raw, small, band_lo)
    return pl.pallas_call(
        functools.partial(finish_kernel, factor),
        out_shape=jax.ShapeDtypeStruct((BINS, 2, nsrc, chans), bf16),
        in_specs=[vmem, vmem, vmem],
        out_specs=hbm,
        scratch_shapes=[
            pltpu.VMEM((2, nsrc, chans), bf16),
            pltpu.SemaphoreType.DMA((3,)),
        ],
        compiler_params=pltpu.CompilerParams(vmem_limit_bytes=32 * 1024 * 1024),
        name="finish",
    )(done, right, left)


def solution(mesh):
    return jax.shard_map(
        functools.partial(per_device, mesh.shape["seg"]),
        mesh=mesh,
        in_specs=(P("chan", "seg"), P(), P(), P(), P()),
        out_specs=P("seg", None, None, "chan"),
        check_vma=False,
    )
```

time: 61.7 us -> 55.7 us (0.903)
  Pallas kernels: 58.8 us -> 52.8 us
  local copies, waits for them, and re-layouts: 2.08 us -> 0.01 us
  other arithmetic: 0.08 us -> 2.07 us
    pallas_call x2, Pallas kernels: 58.8 us -> 52.8 us  [the longest x1 50.9 us: per_device(): pl.pallas_call(functools.partial(kernel, nseg, factor, nsrc, ndead), out_...]
    convert_element_type x0 -> x3, other arithmetic: none -> 2 us  [per_device(): x.astype(f32)]
    unnamed x4 -> x0, local copies, waits for them, and re-layouts: 1.33 us -> none
    rev x1 -> x0, local copies, waits for them, and re-layouts: 0.75 us -> none  [per_device(): fir_taps[::-1].astype(jnp.float32)]
where the time goes in v2:
time: 55.7 us; the launch traced here: 55.6 us
  Pallas kernels  52.8 us (95%)
  other arithmetic  2.07 us (4%)
  between operations  0.66 us (1%)
    pallas_call x1, Pallas kernels, per_device(): pl.pallas_call(functools.partial(kernel, nseg, factor, nsrc, ndead), out_...  50.9 us
    convert_element_type x3, other arithmetic, per_device(): x.astype(f32)  2 us
    pallas_call x1, Pallas kernels, per_device(): pl.pallas_call(functools.partial(finish_kernel, factor), out_shape=jax.Sh...  1.95 us

profile of v2, /device:TPU:1, one launch (start us, length us, event | category | flops | bytes accessed | tf_op | source)
XLA Modules:
  0.0 55.6 jit_solution(5277588470290837821)
XLA Ops:
  0.7 0.7 %convert_element_type.11 = f32[64]{0:T(128)S(1)} convert(s32[64]{0:T(128)} %param.9) | non-fusion elementwise | flops 64 | bytes 512 | tf_op jit(solution)/shard_map/convert_element_type | solution.py:396
  1.3 0.7 %convert_element_type.9 = f32[256]{0:T(256)S(1)} convert(bf16[256]{0:T(256)(128)(2,1)} %param.6) | non-fusion elementwise | flops 256 | bytes 1536 | tf_op jit(solution)/shard_map/convert_element_type | solution.py:396
  2.0 0.7 %convert_element_type.10 = f32[256]{0:T(256)S(1)} convert(s32[256]{0:T(256)} %param.8) | non-fusion elementwise | flops 256 | bytes 2048 | tf_op jit(solution)/shard_map/convert_element_type | solution.py:396
  2.7 0.1 pad_maximum_fusion
  2.7 50.9 %whiten_exchange.1 = (bf16[2,2,256,1280]{3,2,1,0:T(8,128)(2,1)S(1)}, bf16[128,1280]{1,0:T(8,128)(2,1)S(1)}, bf16[128,256]{1,0:T(8,128)(2,1)S(1)}) custom-call(bf16[1280,4096]{1,0:T(8,128)(2,1)} %raw.1, f32[1,640]{1,0:T(1,128)S(1)} %reshape.3.small_ref, s32[1]{0:T(128)S(6)} %copy.6.band_ref), custom_call_target="tpu_custom_call" | custom-call | tf_op jit(solution)/shard_map/whiten_exchange/pallas_call | solution.py:401
  53.6 2.0 %finish.1 = bf16[3,2,256,1280]{3,2,1,0:T(8,128)(2,1)} custom-call(bf16[2,2,256,1280]{3,2,1,0:T(8,128)(2,1)S(1)} %get-tuple-element.8.done_ref, bf16[128,1280]{1,0:T(8,128)(2,1)S(1)} %get-tuple-element.9.right_ref, bf16[128,256]{1,0:T(8,128)(2,1)S(1)} %get-tuple-element.10.left_ref), custom_call_target="tpu_custom_call" | custom-call | tf_op jit(solution)/shard_map/finish/pallas_call | solution.py:445
  (2 shorter events, 0.0 us)

commit v3 on v2

--- a/solution.py
+++ b/solution.py
@@ -38,51 +38,51 @@
     return pltpu.roll(base, 0, 1, stride=DEC, stride_axis=0)
 
 
-def fir_matrix(rolled):
-    rows = []
-    for part in range(BLOCK // 64):
-        pieces = []
-        if part:
-            pieces.append(jnp.zeros((64, 256 * part), jnp.float32))
-        pieces.append(rolled)
-        if part < 3:
-            pieces.append(jnp.zeros((64, 256 * (3 - part)), jnp.float32))
-        rows.append(jnp.concatenate(pieces, axis=1))
-    return jnp.concatenate(rows, axis=0).T.astype(jnp.bfloat16)
+def fir_matrix(rolled, hmat):
+    turned = jnp.concatenate([rolled, jnp.zeros_like(rolled)], axis=0).T
+    later = pltpu.roll(turned, 64, 1)
+    block = jnp.concatenate(
+        [turned[:256], turned[256:] + later[:256], later[256:]], axis=0
+    ).astype(jnp.bfloat16)
+    hmat[0:768, 0:LANE] = block
+    hmat[768:, 0:LANE] = jnp.zeros((SPAN - 768, LANE), jnp.bfloat16)
+    hmat[0:512, LANE:] = jnp.zeros((512, LANE), jnp.bfloat16)
+    hmat[512:, LANE:] = block
 
 
 def dft_table(band_ref, table, nseg):
-    def block(i, _):
-        part = i // BINS
-        freq = band_ref[0] + i % BINS + BINS * lax.broadcasted_iota(jnp.int32, (nseg, LANE), 0)
-        lane = lax.broadcasted_iota(jnp.int32, (nseg, LANE), 1)
-
-        def unit(turn):
-            turn = turn & (NFFT - 1)
-            quad = ((turn + 128) >> 8) & 3
-            rest = ((turn + 128) & 255) - 128
-            x = rest.astype(jnp.float32) * (2.0 * math.pi / NFFT)
-            x2 = x * x
-            sin = x * (1.0 + x2 * (-1.0 / 6 + x2 * (1.0 / 120 + x2 * (-1.0 / 5040 + x2 / 362880))))
-            cos = 1.0 + x2 * (
-                -0.5 + x2 * (1.0 / 24 + x2 * (-1.0 / 720 + x2 * (1.0 / 40320 - x2 / 3628800)))
-            )
-            swap = (quad & 1) == 1
-            c = jnp.where(swap, sin, cos)
-            s = jnp.where(swap, cos, sin)
-            c = jnp.where((quad == 1) | (quad == 2), -c, c)
-            s = jnp.where(quad >= 2, -s, s)
-            return c, s
-
-        c, s = unit(freq * lane + 256 * part)
-        cr, sr = unit(freq * LANE)
-        for a in range(NFFT // LANE):
-            rows = pl.ds(pl.multiple_of(i * nseg, nseg), nseg)
-            table[rows, a * LANE : (a + 1) * LANE] = c.astype(jnp.bfloat16)
-            c, s = c * cr - s * sr, s * cr + c * sr
-        return 0
-
-    lax.fori_loop(0, 2 * BINS, block, 0)
+    def unit(turn):
+        turn = turn & (NFFT - 1)
+        quad = ((turn + 128) >> 8) & 3
+        rest = ((turn + 128) & 255) - 128
+        x = rest.astype(jnp.float32) * (2.0 * math.pi / NFFT)
+        x2 = x * x
+        sin = x * (1.0 + x2 * (-1.0 / 6 + x2 * (1.0 / 120 + x2 * (-1.0 / 5040 + x2 / 362880))))
+        cos = 1.0 + x2 * (
+            -0.5 + x2 * (1.0 / 24 + x2 * (-1.0 / 720 + x2 * (1.0 / 40320 - x2 / 3628800)))
+        )
+        swap = (quad & 1) == 1
+        c = jnp.where(swap, sin, cos)
+        s = jnp.where(swap, cos, sin)
+        c = jnp.where((quad == 1) | (quad == 2), -c, c)
+        s = jnp.where(quad >= 2, -s, s)
+        return c, s
+
+    lane = lax.broadcasted_iota(jnp.int32, (8, LANE), 1)
+    sub = lax.broadcasted_iota(jnp.int32, (8, LANE), 0)
+    for b in range(BINS):
+        for g in range(0, nseg, 16):
+            freq = [band_ref[0] + b + BINS * (sub + g + k) for k in (0, 8)]
+            freq = jnp.concatenate(freq, axis=0)
+            lanes = jnp.concatenate([lane, lane], axis=0)
+            c, s = unit(freq * lanes)
+            cr, sr = unit(freq * LANE)
+            for a in range(NFFT // LANE):
+                at = slice(a * LANE, (a + 1) * LANE)
+                table[b * nseg + g : b * nseg + g + 16, at] = c.astype(jnp.bfloat16)
+                low = (BINS + b) * nseg + g
+                table[low : low + 16, at] = (-s).astype(jnp.bfloat16)
+                c, s = c * cr - s * sr, s * cr + c * sr
 
 
 def products(left, right, factor):
@@ -127,6 +127,7 @@
     half_in,
     half_sum,
     far_in,
+    cross_in,
     total,
     tail_sem,
     raw_sem,
@@ -144,6 +145,7 @@
     core = chan & 1
     sibling = {"chan": chan ^ 1}
     far = {"chan": chan ^ 2}
+    cross = {"chan": chan ^ 3}
     nextseg = {"seg": lax.rem(seg + 1, nseg)}
 
     tail_copy = pltpu.make_async_copy(raw.at[:, pl.ds(samples - TAPS, TAPS)], tail, tail_sem)
@@ -156,7 +158,7 @@
 
     barrier = pltpu.get_barrier_semaphore()
 
-    @pl.loop(1, nseg)
+    @pl.loop(1, nseg, unroll=7)
     def _(d):
         pl.semaphore_signal(
             barrier, 1, device_id={"seg": lax.rem(seg + d, nseg)}, device_id_type=MESH
@@ -164,6 +166,7 @@
 
     pl.semaphore_signal(barrier, 1, device_id=sibling, device_id_type=MESH)
     pl.semaphore_signal(barrier, 1, device_id=far, device_id_type=MESH)
+    pl.semaphore_signal(barrier, 1, device_id=cross, device_id_type=MESH)
 
     rolled = fir_rows(small_ref[:, :TAPS])
     lane64 = lax.broadcasted_iota(jnp.int32, (1, LANE), 1) < 64
@@ -181,7 +184,7 @@
         )
         halo_out[c0 // 2 : c0 // 2 + h] = part.astype(jnp.bfloat16)
 
-    pl.semaphore_wait(barrier, nseg + 1)
+    pl.semaphore_wait(barrier, nseg + 2)
     halos = []
     for q, (c0, w) in enumerate(CHUNKS):
         rows = pl.ds(c0 // 2, w // 2)
@@ -196,7 +199,7 @@
         copy.start()
         halos.append(copy)
 
-    hmat[...] = fir_matrix(rolled)
+    fir_matrix(rolled, hmat)
 
     def filtered(q):
         c0, w = CHUNKS[q]
@@ -227,7 +230,7 @@
     lane = lax.broadcasted_iota(jnp.int32, (1, LANE), 1).astype(jnp.float32)
     alive = []
     for c0 in range(0, chans, LANE):
-        hits = jnp.where(dead == lane + (first_chan + c0), 1.0, 0.0)
+        hits = jnp.where(dead == lane + (first_chan + (c0 + 1)), 1.0, 0.0)
         alive.append(1.0 - jnp.max(hits, axis=0, keepdims=True))
     has_prior = jnp.where(seg > 0, 1.0, 0.0)
     nothing = jnp.zeros((nseg, LANE), jnp.float32)
@@ -238,7 +241,7 @@
         outbox[box] = tiles[box].reshape(nseg, ROWS, LANE).astype(jnp.bfloat16)
         pltpu.make_async_copy(outbox.at[box, seg], inbox.at[box, seg], box_recv.at[box]).start()
 
-        @pl.loop(1, nseg)
+        @pl.loop(1, nseg, unroll=7)
         def _(d):
             to = lax.rem(seg + d, nseg)
             pltpu.make_async_remote_copy(
@@ -327,9 +330,17 @@
         picked[b, 0] = acc[:nseg]
         picked[b, 1] = acc[nseg:]
         exchange(0, b, picked.at[b, 1 - core], half_in.at[b], sibling)
+        if b == BINS - 1:
+            exchange(1, b, picked.at[b, core], far_in.at[b], far)
+            exchange(3, b, picked.at[b, 1 - core], cross_in, cross)
 
     def step_far(b):
         copies[0, b].wait_recv()
+        if b == BINS - 1:
+            half_sum[b] = picked[b, core] + half_in[b]
+            copies[3, b].wait_recv()
+            half_sum[b] = half_sum[b] + cross_in[...]
+            return
         half_sum[b] = picked[b, core] + half_in[b]
         exchange(1, b, half_sum.at[b], far_in.at[b], far)
 
@@ -353,14 +364,16 @@
     collect(2)
     step_pick(1)
     step_far(0)
+    step_far(1)
     collect(3)
     step_pick(2)
-    step_far(1)
+    step_back(0)
+    step_back(1)
+    step_product(0)
     step_far(2)
-    for b in range(BINS):
-        step_back(b)
-    for b in range(BINS):
-        step_product(b)
+    step_back(2)
+    step_product(1)
+    step_product(2)
     for copy in copies.values():
         copy.wait_send()
     for copy in halos:
@@ -392,12 +405,13 @@
     smem = pl.BlockSpec(memory_space=pltpu.SMEM)
     hbm = pl.BlockSpec(memory_space=pltpu.HBM)
     bf16, f32 = jnp.bfloat16, jnp.float32
-    small = jnp.concatenate(
-        [x.astype(f32) for x in (fir_taps, source_chan, dead_chan)]
-        + [jnp.full((LANE - ndead,), -1.0, f32)]
-    ).reshape(1, TAPS + nsrc + LANE)
     nq = len(CHUNKS)
     nbox = 1 + BINS
+    small = (
+        jnp.pad(fir_taps, (0, nsrc + LANE)).astype(f32)
+        + jnp.pad(source_chan, (TAPS, LANE)).astype(f32)
+        + (jnp.pad(dead_chan, (TAPS + nsrc, LANE - ndead), constant_values=-1).astype(f32) + 1.0)
+    ).reshape(1, TAPS + nsrc + LANE)
     done, right, left = pl.pallas_call(
         functools.partial(kernel, nseg, factor, nsrc, ndead),
         out_shape=(
@@ -427,6 +441,7 @@
             pltpu.VMEM((BINS, nseg, nsrc), bf16),
             pltpu.VMEM((BINS, nseg, nsrc), bf16),
             pltpu.VMEM((BINS, nseg, nsrc), bf16),
+            pltpu.VMEM((nseg, nsrc), bf16),
             pltpu.VMEM((BINS, 2, nseg, nsrc), bf16),
             pltpu.SemaphoreType.DMA,
             pltpu.SemaphoreType.DMA((nq,)),
@@ -434,8 +449,8 @@
             pltpu.SemaphoreType.DMA((nq,)),
             pltpu.SemaphoreType.DMA((nbox,)),
             pltpu.SemaphoreType.DMA((nbox,)),
-            pltpu.SemaphoreType.DMA((3, BINS)),
-            pltpu.SemaphoreType.DMA((3, BINS)),
+            pltpu.SemaphoreType.DMA((4, BINS)),
+            pltpu.SemaphoreType.DMA((4, BINS)),
         ],
         compiler_params=pltpu.CompilerParams(
             collective_id=0, has_side_effects=True, vmem_limit_bytes=44 * 1024 * 1024

time: 55.7 us -> 52.5 us (0.943)
  Pallas kernels: 52.8 us -> 51 us
  other arithmetic: 2.07 us -> 0.7 us
    convert_element_type x3 -> x0, other arithmetic: 2 us -> none  [per_device(): x.astype(f32)]
    pallas_call x1, Pallas kernels: 50.9 us -> 49 us  [per_device(): pl.pallas_call(functools.partial(kernel, nseg, factor, nsrc, ndead), out_...]
    add x0 -> x1, other arithmetic: none -> 0.7 us  [per_device(): jnp.pad(fir_taps, (0, nsrc + LANE)).astype(f32)]
where the time goes in v3:
time: 52.5 us; the launch traced here: 52.4 us
  Pallas kernels  51 us (97%)
  other arithmetic  0.7 us (1%)
  between operations  0.66 us (1%)
    pallas_call x1, Pallas kernels, per_device(): pl.pallas_call(functools.partial(kernel, nseg, factor, nsrc, ndead), out_...  49 us
    pallas_call x1, Pallas kernels, per_device(): pl.pallas_call(functools.partial(finish_kernel, factor), out_shape=jax.Sh...  1.95 us

profile of v3, /device:TPU:1, one launch (start us, length us, event | category | flops | bytes accessed | tf_op | source)
XLA Modules:
  0.0 52.4 jit_solution(1089429543802314409)
XLA Ops:
  0.7 0.7 %add_add_fusion = f32[640]{0:T(1024)S(1)} fusion(s32[64]{0:T(128)} %param.9, s32[256]{0:T(256)} %param.8, bf16[256]{0:T(256)(128)(2,1)} %param.6), kind=kLoop, calls=%fused_computation | loop fusion | flops 3840 | bytes 4352 | tf_op jit(solution)/shard_map/add | solution.py:411
  1.4 49.0 %whiten_exchange.1 = (bf16[2,2,256,1280]{3,2,1,0:T(8,128)(2,1)S(1)}, bf16[128,1280]{1,0:T(8,128)(2,1)S(1)}, bf16[128,256]{1,0:T(8,128)(2,1)S(1)}) custom-call(bf16[1280,4096]{1,0:T(8,128)(2,1)} %raw.1, f32[1,640]{1,0:T(1,128)S(1)} %reshape.3.small_ref, s32[1]{0:T(128)S(6)} %copy.6.band_ref), custom_call_target="tpu_custom_call" | custom-call | tf_op jit(solution)/shard_map/whiten_exchange/pallas_call | solution.py:415
  50.4 2.0 %finish.1 = bf16[3,2,256,1280]{3,2,1,0:T(8,128)(2,1)} custom-call(bf16[2,2,256,1280]{3,2,1,0:T(8,128)(2,1)S(1)} %get-tuple-element.8.done_ref, bf16[128,1280]{1,0:T(8,128)(2,1)S(1)} %get-tuple-element.9.right_ref, bf16[128,256]{1,0:T(8,128)(2,1)S(1)} %get-tuple-element.10.left_ref), custom_call_target="tpu_custom_call" | custom-call | tf_op jit(solution)/shard_map/finish/pallas_call | solution.py:460
  (1 shorter events, 0.0 us)

commit v4 on v3

--- a/solution.py
+++ b/solution.py
@@ -158,15 +158,16 @@
 
     barrier = pltpu.get_barrier_semaphore()
 
-    @pl.loop(1, nseg, unroll=7)
-    def _(d):
-        pl.semaphore_signal(
-            barrier, 1, device_id={"seg": lax.rem(seg + d, nseg)}, device_id_type=MESH
-        )
-
     pl.semaphore_signal(barrier, 1, device_id=sibling, device_id_type=MESH)
     pl.semaphore_signal(barrier, 1, device_id=far, device_id_type=MESH)
     pl.semaphore_signal(barrier, 1, device_id=cross, device_id_type=MESH)
+
+    @pl.loop(1, nseg, unroll=21)
+    def _(d):
+        pl.semaphore_signal(
+            barrier, 1, device_id={"seg": seg ^ (nseg - d)}, device_id_type=MESH
+        )
+
 
     rolled = fir_rows(small_ref[:, :TAPS])
     lane64 = lax.broadcasted_iota(jnp.int32, (1, LANE), 1) < 64
@@ -241,7 +242,7 @@
         outbox[box] = tiles[box].reshape(nseg, ROWS, LANE).astype(jnp.bfloat16)
         pltpu.make_async_copy(outbox.at[box, seg], inbox.at[box, seg], box_recv.at[box]).start()
 
-        @pl.loop(1, nseg, unroll=7)
+        @pl.loop(1, nseg, unroll=21)
         def _(d):
             to = lax.rem(seg + d, nseg)
             pltpu.make_async_remote_copy(

time: 52.5 us -> 52.1 us (level)
  no operation moved by 1% of the time
where the time goes in v4:
time: 52.1 us; the launch traced here: 52 us
  Pallas kernels  50.6 us (97%)
  other arithmetic  0.7 us (1%)
  between operations  0.66 us (1%)
    pallas_call x1, Pallas kernels, per_device(): pl.pallas_call(functools.partial(kernel, nseg, factor, nsrc, ndead), out_...  48.6 us
    pallas_call x1, Pallas kernels, per_device(): pl.pallas_call(functools.partial(finish_kernel, factor), out_shape=jax.Sh...  1.95 us

profile of v4, /device:TPU:1, one launch (start us, length us, event | category | flops | bytes accessed | tf_op | source)
XLA Modules:
  0.0 52.0 jit_solution(1808288481788128105)
XLA Ops:
  0.7 0.7 %add_add_fusion = f32[640]{0:T(1024)S(1)} fusion(s32[64]{0:T(128)} %param.9, s32[256]{0:T(256)} %param.8, bf16[256]{0:T(256)(128)(2,1)} %param.6), kind=kLoop, calls=%fused_computation | loop fusion | flops 3840 | bytes 4352 | tf_op jit(solution)/shard_map/add | solution.py:412
  1.4 48.6 %whiten_exchange.1 = (bf16[2,2,256,1280]{3,2,1,0:T(8,128)(2,1)S(1)}, bf16[128,1280]{1,0:T(8,128)(2,1)S(1)}, bf16[128,256]{1,0:T(8,128)(2,1)S(1)}) custom-call(bf16[1280,4096]{1,0:T(8,128)(2,1)} %raw.1, f32[1,640]{1,0:T(1,128)S(1)} %reshape.3.small_ref, s32[1]{0:T(128)S(6)} %copy.6.band_ref), custom_call_target="tpu_custom_call" | custom-call | tf_op jit(solution)/shard_map/whiten_exchange/pallas_call | solution.py:416
  50.0 2.0 %finish.1 = bf16[3,2,256,1280]{3,2,1,0:T(8,128)(2,1)} custom-call(bf16[2,2,256,1280]{3,2,1,0:T(8,128)(2,1)S(1)} %get-tuple-element.8.done_ref, bf16[128,1280]{1,0:T(8,128)(2,1)S(1)} %get-tuple-element.9.right_ref, bf16[128,256]{1,0:T(8,128)(2,1)S(1)} %get-tuple-element.10.left_ref), custom_call_target="tpu_custom_call" | custom-call | tf_op jit(solution)/shard_map/finish/pallas_call | solution.py:461
  (1 shorter events, 0.0 us)

commit v5 on v4

--- a/solution.py
+++ b/solution.py
@@ -326,7 +326,12 @@
         copies[step, b] = copy
 
     def step_pick(b):
-        acc = jnp.dot(right_of(b)[...], hot[...], preferred_element_type=jnp.float32)
+        if b == BINS - 1:
+            acc = early + jnp.dot(
+                right_last[:, :1024], hot[:1024], preferred_element_type=jnp.float32
+            )
+        else:
+            acc = jnp.dot(right_of(b)[...], hot[...], preferred_element_type=jnp.float32)
         acc = acc.astype(jnp.bfloat16)
         picked[b, 0] = acc[:nseg]
         picked[b, 1] = acc[nseg:]
@@ -360,6 +365,7 @@
             done_ref[b, part] = value
 
     collect(0)
+    early = jnp.dot(right_last[:, 1024:], hot[1024:], preferred_element_type=jnp.float32)
     collect(1)
     step_pick(0)
     collect(2)

time: 52.1 us -> 52.1 us (level)
  no operation moved by 1% of the time
where the time goes in v5:
time: 52.1 us; the launch traced here: 52 us
  Pallas kernels  50.6 us (97%)
  other arithmetic  0.7 us (1%)
  between operations  0.66 us (1%)
    pallas_call x1, Pallas kernels, per_device(): pl.pallas_call(functools.partial(kernel, nseg, factor, nsrc, ndead), out_...  48.6 us
    pallas_call x1, Pallas kernels, per_device(): pl.pallas_call(functools.partial(finish_kernel, factor), out_shape=jax.Sh...  1.95 us

profile of v5, /device:TPU:1, one launch (start us, length us, event | category | flops | bytes accessed | tf_op | source)
XLA Modules:
  0.0 52.0 jit_solution(11488428114532372030)
XLA Ops:
  0.7 0.7 %add_add_fusion = f32[640]{0:T(1024)S(1)} fusion(s32[64]{0:T(128)} %param.9, s32[256]{0:T(256)} %param.8, bf16[256]{0:T(256)(128)(2,1)} %param.6), kind=kLoop, calls=%fused_computation | loop fusion | flops 3840 | bytes 4352 | tf_op jit(solution)/shard_map/add | solution.py:418
  1.4 48.6 %whiten_exchange.1 = (bf16[2,2,256,1280]{3,2,1,0:T(8,128)(2,1)S(1)}, bf16[128,1280]{1,0:T(8,128)(2,1)S(1)}, bf16[128,256]{1,0:T(8,128)(2,1)S(1)}) custom-call(bf16[1280,4096]{1,0:T(8,128)(2,1)} %raw.1, f32[1,640]{1,0:T(1,128)S(1)} %reshape.3.small_ref, s32[1]{0:T(128)S(6)} %copy.6.band_ref), custom_call_target="tpu_custom_call" | custom-call | tf_op jit(solution)/shard_map/whiten_exchange/pallas_call | solution.py:422
  50.0 2.0 %finish.1 = bf16[3,2,256,1280]{3,2,1,0:T(8,128)(2,1)} custom-call(bf16[2,2,256,1280]{3,2,1,0:T(8,128)(2,1)S(1)} %get-tuple-element.8.done_ref, bf16[128,1280]{1,0:T(8,128)(2,1)S(1)} %get-tuple-element.9.right_ref, bf16[128,256]{1,0:T(8,128)(2,1)S(1)} %get-tuple-element.10.left_ref), custom_call_target="tpu_custom_call" | custom-call | tf_op jit(solution)/shard_map/finish/pallas_call | solution.py:467
  (1 shorter events, 0.0 us)
